TPU v7x, 32 devices: a whole 2x2x4 slice. The times are simulated.
32 devices in a mesh: inst: 4 (over x, core), stream: 4 (over z), rad: 2 (over y).
Axes of the slice: x: 2, y: 2, z: 4, core: 2. Of those that a mesh axis runs over, the one named last changes fastest.
Arguments:
- state: float32 [4, 6, 64, 32, 128], P('inst', None, 'stream', 'rad'), may hold values from -6 to 6
- axial_speed: float32 [64, 32, 128], P('stream', 'rad'), may hold values from 0.5 to 1.5
- cross_speed: float32 [2, 64, 32, 128], P(None, 'stream', 'rad'), may hold values from -0.5 to 0.5
- viscosity: float32 [64, 32, 128], P('stream', 'rad'), may hold values from 0.01 to 0.2
- coupling: float32 [6, 6], replicated, may hold values from -1.5 to 1.5
- targets: int32 [4, 32, 128, 2], P('inst', 'rad'), may hold values from 0 to 511
- shares: float32 [4, 32, 128], P('inst', 'rad'), may hold values from 0.2 to 0.8
Outputs:
- updated: float32 [4, 6, 64, 32, 128], P('inst', None, 'stream', 'rad')
Inputs may be any that keep to these rules, and one draw needn't show every extreme that they name: targets[n, r, j, k] = m * 128 + t names slot t of the stator face of instance m.
All inputs are finite; a program needn't handle non-finite values.
Results may differ from a plain program's by a relative error of at most 0.0001.
Values sent between devices are 32-bit elements; how exact they have to be, the bound alone decides.
A program may use at most 64 MiB of HBM per device.

v0:
```python
import jax
import jax.numpy as jnp
from jax import lax
from jax.sharding import PartitionSpec as P

omega_scale = 0.5
pseudo_step = 0.5


def shifted(value, axis, steps):
    count = lax.axis_size(axis)
    pairs = [(source, (source + steps) % count) for source in range(count)]
    return lax.ppermute(value, axis, pairs)


def with_halo(block, sides, width):
    for axis, dim in sides:
        count = lax.axis_size(axis)
        forward = [(i, i + 1) for i in range(count - 1)]
        backward = [(target, source) for source, target in forward]
        low = lax.ppermute(
            lax.slice_in_dim(block, block.shape[dim] - width, None, axis=dim), axis, forward
        )
        high = lax.ppermute(lax.slice_in_dim(block, 0, width, axis=dim), axis, backward)
        block = jnp.concatenate([low, block, high], axis=dim)
    return block


def coefficient(steps, count):
    kf = steps.astype(jnp.float32)
    safe = jnp.where(steps == 0, jnp.ones_like(kf), kf)
    sign = 1.0 - 2.0 * jnp.mod(safe, 2.0)
    angle = jnp.pi * safe / count
    value = omega_scale * 0.5 * sign * jnp.cos(angle) / jnp.sin(angle)
    return jnp.where(steps == 0, jnp.zeros_like(value), value)


def spectral(field):
    count = lax.axis_size("inst")

    def turn(step, carry):
        visiting, total = carry
        visiting = shifted(visiting, "inst", 1)
        return (visiting, total + coefficient(step, count) * visiting)

    moved, total = lax.fori_loop(1, count, turn, (field, jnp.zeros_like(field)))
    return total


def split_values(face_flux, shares):
    weights = jnp.stack([shares, 1.0 - shares], axis=-1)
    return face_flux[..., None] * weights[None]


def sender_inflow(upstream_face, targets, shares):
    count = lax.axis_size("inst")
    width = upstream_face.shape[2]
    columns = jnp.arange(count * width, dtype=jnp.int32)
    values = jnp.transpose(split_values(upstream_face, shares), (1, 0, 2, 3))

    def one_row(args):
        row_values, row_targets = args
        onehot = (row_targets[..., None] == columns).astype(jnp.float32)
        return jnp.einsum("vjk,jkc->vc", row_values, onehot, precision=lax.Precision.HIGHEST)

    blocks = lax.map(one_row, (values, targets))
    blocks = blocks.reshape(blocks.shape[0], blocks.shape[1], count, width)
    blocks = jnp.transpose(blocks, (2, 1, 0, 3))
    arrived = lax.all_to_all(blocks, "inst", split_axis=0, concat_axis=0, tiled=True)
    return jnp.sum(arrived, axis=0)


def operator(field, axial_speed, cross_speed, viscosity, coupling, targets, shares):
    plain = field[0]
    nvars = plain.shape[0]
    flux = axial_speed[None] * plain
    stacked = jnp.concatenate([plain, flux], axis=0)
    padded = with_halo(stacked, (("stream", 1), ("rad", 2)), 1)
    s_low = padded[:nvars, :-2, 1:-1]
    s_high = padded[:nvars, 2:, 1:-1]
    r_low = padded[:nvars, 1:-1, :-2]
    r_high = padded[:nvars, 1:-1, 2:]
    up_flux = padded[nvars:, :-2, 1:-1]
    upstream_face = padded[nvars:, 0, 1:-1]
    inflow = sender_inflow(upstream_face, targets[0], shares[0])
    stator_first = lax.axis_index("stream") == lax.axis_size("stream") // 2
    first = jnp.where(stator_first, inflow, up_flux[:, 0])
    up_flux = jnp.concatenate([first[:, None], up_flux[:, 1:]], axis=1)
    t_low = jnp.roll(plain, 1, axis=3)
    t_high = jnp.roll(plain, -1, axis=3)
    radial = cross_speed[0][None]
    beside_all = cross_speed[1][None]
    advect = jnp.maximum(radial, 0.0) * (plain - r_low) + jnp.minimum(radial, 0.0) * (
        r_high - plain
    )
    advect = (
        advect
        + jnp.maximum(beside_all, 0.0) * (plain - t_low)
        + jnp.minimum(beside_all, 0.0) * (t_high - plain)
    )
    neighbours = s_low + s_high + r_low + r_high + t_low + t_high
    diffuse = viscosity[None] * (neighbours - 6.0 * plain)
    source = jnp.einsum("vw,wsrt->vsrt", coupling, plain, precision=lax.Precision.HIGHEST)
    return (flux - up_flux + advect - diffuse + source)[None]


def body(state, axial_speed, cross_speed, viscosity, coupling, targets, shares):

    def total(field):
        return spectral(field) + operator(
            field, axial_speed, cross_speed, viscosity, coupling, targets, shares
        )

    middle = state - 0.5 * pseudo_step * total(state)
    return state - pseudo_step * total(middle)


def solution(mesh):
    in_specs = (
        P("inst", None, "stream", "rad", None),
        P("stream", "rad", None),
        P(None, "stream", "rad", None),
        P("stream", "rad", None),
        P(),
        P("inst", "rad", None, None),
        P("inst", "rad", None),
    )
    out_specs = P("inst", None, "stream", "rad", None)
    return jax.shard_map(body, mesh=mesh, in_specs=in_specs, out_specs=out_specs, check_vma=False)
```

profile of v0, /device:TPU:16, one launch (start us, length us, event | category | flops | bytes accessed | tf_op | source)
XLA Modules:
  0.0 204.1 jit_solution(18268516859020818549)
XLA Ops:
  0.0 1.4 broadcast_multiply_fusion.1
  2.4 2.3 %collective-permute-start.3 = (f32[12,1,16,128]{3,2,1,0:T(8,128)}, f32[12,1,16,128]{3,2,1,0:T(8,128)}, u32[]{:S(2)}, u32[]{:S(2)}) collective-permute-start(f32[12,1,16,128]{3,2,1,0:T(8,128)} %get-tuple-element.281), channel_id=1, source_target_pairs={{2,0},{4,2},{6,4},{3,1},{5,3},{7,5},{10,8},{12,10},{14,12},{11,9},... | collective-permute-start | bytes 294920 | tf_op jit(solution)/shard_map/ppermute | solution.py:24
  4.7 4.1 %collective-permute-start.2 = (f32[12,1,16,128]{3,2,1,0:T(8,128)S(1)}, f32[12,1,16,128]{3,2,1,0:T(8,128)S(1)}, u32[]{:S(2)}, u32[]{:S(2)}) collective-permute-start(f32[12,1,16,128]{3,2,1,0:T(8,128)S(1)} %get-tuple-element.280), channel_id=1, source_target_pairs={{0,2},{2,4},{4,6},{1,3},{3,5},{5,7},{8,10},{10,12},{12,14},{9,11},... | collective-permute-start | bytes 294920 | tf_op jit(solution)/shard_map/ppermute | solution.py:21
  8.8 1.4 fusion.65
  10.2 1.4 fusion.66
  11.6 2.4 %fusion.16 = f32[6,16,16,128]{3,0,2,1:T(8,128)} fusion(f32[6,16,16,128]{3,2,1,0:T(8,128)S(1)} %bitcast.92, f32[6,6]{1,0:T(8,128)S(1)} %copy-done), kind=kOutput, calls=%fused_computation.22 | convolution fusion | flops 14155776 | bytes 1573008 | tf_op jit(solution)/shard_map/vw,wsrt->vsrt/dot_general | solution.py:103
  14.7 16.3 %while.54 = (s32[]{:T(128)}, f32[16,6,512]{2,1,0:T(8,128)S(1)}, f32[16,6,128,2]{2,1,3,0:T(8,128)S(1)}, s32[16,128,2]{1,2,0:T(2,128)}, s32[]{:T(128)}) while((s32[]{:T(128)}, f32[16,6,512]{2,1,0:T(8,128)S(1)}, f32[16,6,128,2]{2,1,3,0:T(8,128)S(1)}, s32[16,128,2]{1,2,0:T(2,128)}, s32[]{:T(128)}) %tuple.119), condition=%wide.region_3.4_spmd.clone, body=%wide.region_2.3_spmd.clone.sunk | while | flops 9568258 | bytes 28745 | solution.py:66
  31.8 4.1 %all-to-all-start = ((f32[4,6,16,128]{3,2,1,0:T(8,128)}), f32[4,6,16,128]{3,2,1,0:T(8,128)}, u32[]{:S(2)}, u32[]{:S(2)}) async-start(f32[4,6,16,128]{3,2,1,0:T(8,128)} %copy.45), calls=%async_computation | async-start | bytes 393216 | tf_op jit(solution)/shard_map/all_to_all | solution.py:69
  37.6 1.7 pad_maximum_fusion.35
  40.6 5.9 %collective-permute-start.4 = (f32[12,18,1,128]{3,2,1,0:T(1,128)}, f32[12,18,1,128]{3,2,1,0:T(1,128)}, u32[]{:S(2)}, u32[]{:S(2)}) collective-permute-start(f32[12,18,1,128]{3,2,1,0:T(1,128)} %get-tuple-element.276), channel_id=1, source_target_pairs={{0,1},{2,3},{4,5},{6,7},{8,9},{10,11},{12,13},{14,15},{16,17},{18,... | collective-permute-start | bytes 331784 | tf_op jit(solution)/shard_map/ppermute | solution.py:21
  48.1 38.0 %while.56 = (s32[]{:T(128)}, f32[1,6,16,16,128]{4,3,2,1,0:T(8,128)S(1)}, f32[1,6,16,16,128]{4,3,2,1,0:T(8,128)}, s32[]{:T(128)}, s32[]{:T(128)}, /*index=5*/f32[...) while((s32[]{:T(128)}, f32[1,6,16,16,128]{4,3,2,1,0:T(8,128)S(1)}, ...), condition=%wide.region_1.2_spmd.clone, body=%wide.region_0.1_spmd.clone.sunk | while | flops 589843 | bytes 13369752 | solution.py:46
  48.4 11.1 %collective-permute-done = f32[1,6,16,16,128]{4,3,2,1,0:T(8,128)S(1)} collective-permute-done((f32[1,6,16,16,128]{4,3,2,1,0:T(8,128)S(1)}, f32[1,6,16,16,128]{4,3,2,1,0:T(8,128)S(1)}, u32[]{:S(2)}, u32[]{:S(2)}) %collective-permute-start) | collective-permute-done | bytes 786464 | tf_op jit(solution)/shard_map/while/body/eval_jaxpr/ppermute | solution.py:13
  61.0 11.1 %collective-permute-done = f32[1,6,16,16,128]{4,3,2,1,0:T(8,128)S(1)} collective-permute-done((f32[1,6,16,16,128]{4,3,2,1,0:T(8,128)S(1)}, f32[1,6,16,16,128]{4,3,2,1,0:T(8,128)S(1)}, u32[]{:S(2)}, u32[]{:S(2)}) %collective-permute-start) | collective-permute-done | bytes 786464 | tf_op jit(solution)/shard_map/while/body/eval_jaxpr/ppermute | solution.py:13
  73.7 11.1 %collective-permute-done = f32[1,6,16,16,128]{4,3,2,1,0:T(8,128)S(1)} collective-permute-done((f32[1,6,16,16,128]{4,3,2,1,0:T(8,128)S(1)}, f32[1,6,16,16,128]{4,3,2,1,0:T(8,128)S(1)}, u32[]{:S(2)}, u32[]{:S(2)}) %collective-permute-start) | collective-permute-done | bytes 786464 | tf_op jit(solution)/shard_map/while/body/eval_jaxpr/ppermute | solution.py:13
  86.1 4.2 %broadcast_multiply_fusion = (f32[6,16,16,128]{3,2,1,0:T(8,128)S(1)}, f32[1,6,16,16,128]{4,3,2,1,0:T(8,128)S(1)}) fusion(f32[16,16,128]{2,1,0:T(8,128)} %param.16, f32[1,6,16,16,128]{4,3,2,1,0:T(8,128)S(1)} %copy-done.1, f32[1,6,16,16,128]{4,3,2,1,0:T(8,128)} %get-tuple-element.187, f32[6,16,16,128]{3,0,2,1:T(8,128)} %fusion.16, ...), kind=kLoop, calls=%fused_computation.96 | loop fusion | flops 8257536 | bytes 9068544 | tf_op jit(solution)/shard_map/mul | solution.py:76
  90.3 1.4 fusion.63
  92.3 1.9 collective-permute-start.6
  94.2 1.4 fusion.64
  95.6 3.9 %collective-permute-start.7 = (f32[12,1,16,128]{3,2,1,0:T(8,128)}, f32[12,1,16,128]{3,2,1,0:T(8,128)}, u32[]{:S(2)}, u32[]{:S(2)}) collective-permute-start(f32[12,1,16,128]{3,2,1,0:T(8,128)} %get-tuple-element.279), channel_id=1, source_target_pairs={{2,0},{4,2},{6,4},{3,1},{5,3},{7,5},{10,8},{12,10},{14,12},{11,9},... | collective-permute-start | bytes 294920 | tf_op jit(solution)/shard_map/ppermute | solution.py:24
  101.7 37.0 %while.55 = (s32[]{:T(128)}, f32[16,6,512]{2,1,0:T(8,128)}, f32[16,6,128,2]{2,1,3,0:T(8,128)}, s32[16,128,2]{1,2,0:T(2,128)}, s32[]{:T(128)}) while((s32[]{:T(128)}, f32[16,6,512]{2,1,0:T(8,128)}, f32[16,6,128,2]{2,1,3,0:T(8,128)}, s32[16,128,2]{1,2,0:T(2,128)}, s32[]{:T(128)}) %tuple.120), condition=%wide.region_8.9_spmd.clone, body=%wide.region_7.8_spmd.clone.sunk | while | flops 9568258 | bytes 28745 | solution.py:66
  102.4 1.6 fusion.74
  104.7 1.6 fusion.74
  107.0 1.6 fusion.74
  109.4 1.6 fusion.74
  111.7 1.6 fusion.74
  114.0 1.6 fusion.74
  116.3 1.6 fusion.74
  118.6 1.6 fusion.74
  120.9 1.6 fusion.74
  123.2 1.6 fusion.74
  125.6 1.6 fusion.74
  127.9 1.6 fusion.74
  130.2 1.6 fusion.74
  132.5 1.6 fusion.74
  134.8 1.6 fusion.74
  137.1 1.6 fusion.74
  138.8 1.7 reshape.35
  140.5 1.7 copy.51
  142.1 4.0 %all-to-all-start.1 = ((f32[4,6,16,128]{3,2,1,0:T(8,128)}), f32[4,6,16,128]{3,2,1,0:T(8,128)}, u32[]{:S(2)}, u32[]{:S(2)}) async-start(f32[4,6,16,128]{3,2,1,0:T(8,128)} %copy.51), calls=%async_computation.1 | async-start | bytes 393216 | tf_op jit(solution)/shard_map/all_to_all | solution.py:69
  146.1 2.4 %fusion.14 = f32[16,16,128,6]{2,3,1,0:T(8,128)} fusion(f32[6,16,16,128]{3,2,1,0:T(8,128)S(1)} %bitcast.98, f32[6,6]{1,0:T(8,128)S(1)} %copy-done), kind=kOutput, calls=%fused_computation.20 | convolution fusion | flops 14155776 | bytes 1573008 | tf_op jit(solution)/shard_map/vw,wsrt->vsrt/dot_general | solution.py:103
  150.4 1.7 pad_maximum_fusion.31
  152.0 1.3 collective-permute-start.9
  153.3 5.9 %collective-permute-start.8 = (f32[12,18,1,128]{3,2,1,0:T(1,128)}, f32[12,18,1,128]{3,2,1,0:T(1,128)}, u32[]{:S(2)}, u32[]{:S(2)}) collective-permute-start(f32[12,18,1,128]{3,2,1,0:T(1,128)} %get-tuple-element.274), channel_id=1, source_target_pairs={{0,1},{2,3},{4,5},{6,7},{8,9},{10,11},{12,13},{14,15},{16,17},{18,... | collective-permute-start | bytes 331784 | tf_op jit(solution)/shard_map/ppermute | solution.py:21
  160.9 38.4 %while.57 = (s32[]{:T(128)}, f32[1,6,16,16,128]{4,3,2,1,0:T(8,128)}, f32[1,6,16,16,128]{4,3,2,1,0:T(8,128)S(1)}, s32[]{:T(128)}, s32[]{:T(128)}, /*index=5*/f32[...) while((s32[]{:T(128)}, f32[1,6,16,16,128]{4,3,2,1,0:T(8,128)}, ...), condition=%wide.region_6.7_spmd.clone, body=%wide.region_5.6_spmd.clone.sunk | while | flops 589843 | bytes 7078240 | solution.py:46
  161.1 11.4 %collective-permute-done.1 = f32[1,6,16,16,128]{4,3,2,1,0:T(8,128)S(1)} collective-permute-done((f32[1,6,16,16,128]{4,3,2,1,0:T(8,128)}, f32[1,6,16,16,128]{4,3,2,1,0:T(8,128)S(1)}, u32[]{:S(2)}, u32[]{:S(2)}) %collective-permute-start.1) | collective-permute-done | bytes 786464 | tf_op jit(solution)/shard_map/while/body/eval_jaxpr/ppermute | solution.py:13
  174.0 11.4 %collective-permute-done.1 = f32[1,6,16,16,128]{4,3,2,1,0:T(8,128)S(1)} collective-permute-done((f32[1,6,16,16,128]{4,3,2,1,0:T(8,128)}, f32[1,6,16,16,128]{4,3,2,1,0:T(8,128)S(1)}, u32[]{:S(2)}, u32[]{:S(2)}) %collective-permute-start.1) | collective-permute-done | bytes 786464 | tf_op jit(solution)/shard_map/while/body/eval_jaxpr/ppermute | solution.py:13
  186.8 11.4 %collective-permute-done.1 = f32[1,6,16,16,128]{4,3,2,1,0:T(8,128)S(1)} collective-permute-done((f32[1,6,16,16,128]{4,3,2,1,0:T(8,128)}, f32[1,6,16,16,128]{4,3,2,1,0:T(8,128)S(1)}, u32[]{:S(2)}, u32[]{:S(2)}) %collective-permute-start.1) | collective-permute-done | bytes 786464 | tf_op jit(solution)/shard_map/while/body/eval_jaxpr/ppermute | solution.py:13
  199.3 4.8 %fusion.30 = f32[1,6,16,16,128]{4,3,2,1,0:T(8,128)} fusion(f32[1,6,16,16,128]{4,3,2,1,0:T(8,128)S(1)} %copy-done.1, f32[1,6,16,16,128]{4,3,2,1,0:T(8,128)S(1)} %get-tuple-element.189, f32[12,1,16,128]{3,2,1,0:T(8,128)} %collective-permute-done.7, f32[6,16,16,128]{3,2,1,0:T(8,128)} %copy-done.5, f32[6,16,16,128]{3,2,1,0:T(8,128)S(1)} %bitcast.100, ...), kind=kLoop, calls=%fused_computation.37 | loop fusion | flops 8060928 | bytes 8151040 | tf_op jit(solution)/shard_map/sub | solution.py:115
  (142 shorter events, 47.4 us)
Async XLA Ops:
  0.0 11.6 %copy-start = (f32[6,6]{1,0:T(8,128)S(1)}, f32[6,6]{1,0:T(8,128)}, u32[]{:S(2)}) copy-start(f32[6,6]{1,0:T(8,128)} %param.19) | copy-start | bytes 436
  0.0 1.4 copy-start.2
  0.0 1.7 copy-start.1
  1.4 36.1 %copy-start.6 = (f32[6,16,16,128]{3,2,1,0:T(8,128)}, f32[6,16,16,128]{3,2,1,0:T(8,128)S(1)}, u32[]{:S(2)}) copy-start(f32[6,16,16,128]{3,2,1,0:T(8,128)S(1)} %broadcast_multiply_fusion.1) | copy-start | bytes 2359300
  2.4 35.2 %collective-permute-start.3 = (f32[12,1,16,128]{3,2,1,0:T(8,128)}, f32[12,1,16,128]{3,2,1,0:T(8,128)}, u32[]{:S(2)}, u32[]{:S(2)}) collective-permute-start(f32[12,1,16,128]{3,2,1,0:T(8,128)} %get-tuple-element.281), channel_id=1, source_target_pairs={{2,0},{4,2},{6,4},{3,1},{5,3},{7,5},{10,8},{12,10},{14,12},{11,9},... | collective-permute-start | bytes 294920 | tf_op jit(solution)/shard_map/ppermute | solution.py:24
  4.7 9.3 %collective-permute-start.2 = (f32[12,1,16,128]{3,2,1,0:T(8,128)S(1)}, f32[12,1,16,128]{3,2,1,0:T(8,128)S(1)}, u32[]{:S(2)}, u32[]{:S(2)}) collective-permute-start(f32[12,1,16,128]{3,2,1,0:T(8,128)S(1)} %get-tuple-element.280), channel_id=1, source_target_pairs={{0,2},{2,4},{4,6},{1,3},{3,5},{5,7},{8,10},{10,12},{12,14},{9,11},... | collective-permute-start | bytes 294920 | tf_op jit(solution)/shard_map/ppermute | solution.py:21
  11.6 2.4 %copy-start.15 = (f32[1,16,128]{2,1,0:T(8,128)S(1)}, f32[1,16,128]{2,1,0:T(8,128)}, u32[]{:S(2)}) copy-start(f32[1,16,128]{2,1,0:T(8,128)} %param.21) | copy-start | bytes 24580
  14.0 0.6 copy-start.13
  14.0 0.6 copy-start.7
  31.8 4.1 %copy-start.12 = (f32[2,16,16,128]{3,2,1,0:T(8,128)S(1)}, f32[2,16,16,128]{3,2,1,0:T(8,128)}, u32[]{:S(2)}) copy-start(f32[2,16,16,128]{3,2,1,0:T(8,128)} %param.17) | copy-start | bytes 786436
  31.8 14.7 %all-to-all-start = ((f32[4,6,16,128]{3,2,1,0:T(8,128)}), f32[4,6,16,128]{3,2,1,0:T(8,128)}, u32[]{:S(2)}, u32[]{:S(2)}) async-start(f32[4,6,16,128]{3,2,1,0:T(8,128)} %copy.45), calls=%async_computation | async-start | bytes 393216 | tf_op jit(solution)/shard_map/all_to_all | solution.py:69
  39.3 46.8 %collective-permute-start.5 = (f32[12,18,1,128]{3,2,1,0:T(1,128)}, f32[12,18,1,128]{3,2,1,0:T(1,128)}, u32[]{:S(2)}, u32[]{:S(2)}) collective-permute-start(f32[12,18,1,128]{3,2,1,0:T(1,128)} %get-tuple-element.277), channel_id=1, source_target_pairs={{1,0},{3,2},{5,4},{7,6},{9,8},{11,10},{13,12},{15,14},{17,16},{19,... | collective-permute-start | bytes 331784 | tf_op jit(solution)/shard_map/ppermute | solution.py:24
  40.6 6.9 %copy-start.8 = (f32[12,1,16,128]{3,2,1,0:T(8,128)S(1)}, f32[12,1,16,128]{3,2,1,0:T(8,128)}, u32[]{:S(2)}) copy-start(f32[12,1,16,128]{3,2,1,0:T(8,128)} %copy-done.7) | copy-start | bytes 294916
  40.6 45.5 %collective-permute-start.4 = (f32[12,18,1,128]{3,2,1,0:T(1,128)}, f32[12,18,1,128]{3,2,1,0:T(1,128)}, u32[]{:S(2)}, u32[]{:S(2)}) collective-permute-start(f32[12,18,1,128]{3,2,1,0:T(1,128)} %get-tuple-element.276), channel_id=1, source_target_pairs={{0,1},{2,3},{4,5},{6,7},{8,9},{10,11},{12,13},{14,15},{16,17},{18,... | collective-permute-start | bytes 331784 | tf_op jit(solution)/shard_map/ppermute | solution.py:21
  48.1 11.4 %collective-permute-start = (f32[1,6,16,16,128]{4,3,2,1,0:T(8,128)S(1)}, f32[1,6,16,16,128]{4,3,2,1,0:T(8,128)S(1)}, u32[]{:S(2)}, u32[]{:S(2)}) collective-permute-start(f32[1,6,16,16,128]{4,3,2,1,0:T(8,128)S(1)} %get-tuple-element.393), channel_id=1, source_target_pairs={{0,8},{8,16},{16,24},{24,0},{1,9},{9,17},{17,25},{25,1},{2,10},{10... | collective-permute-start | bytes 2359304 | tf_op jit(solution)/shard_map/while/body/eval_jaxpr/ppermute | solution.py:13
  48.4 11.2 %copy-start.3 = (f32[1,6,16,16,128]{4,3,2,1,0:T(8,128)S(1)}, f32[1,6,16,16,128]{4,3,2,1,0:T(8,128)}, u32[]{:S(2)}) copy-start(f32[1,6,16,16,128]{4,3,2,1,0:T(8,128)} %get-tuple-element.394) | copy-start | bytes 2359300 | tf_op jit(solution)/shard_map/while
  59.9 0.9 copy-start.4
  60.8 11.4 %collective-permute-start = (f32[1,6,16,16,128]{4,3,2,1,0:T(8,128)S(1)}, f32[1,6,16,16,128]{4,3,2,1,0:T(8,128)S(1)}, u32[]{:S(2)}, u32[]{:S(2)}) collective-permute-start(f32[1,6,16,16,128]{4,3,2,1,0:T(8,128)S(1)} %get-tuple-element.393), channel_id=1, source_target_pairs={{0,8},{8,16},{16,24},{24,0},{1,9},{9,17},{17,25},{25,1},{2,10},{10... | collective-permute-start | bytes 2359304 | tf_op jit(solution)/shard_map/while/body/eval_jaxpr/ppermute | solution.py:13
  61.0 11.2 %copy-start.3 = (f32[1,6,16,16,128]{4,3,2,1,0:T(8,128)S(1)}, f32[1,6,16,16,128]{4,3,2,1,0:T(8,128)}, u32[]{:S(2)}) copy-start(f32[1,6,16,16,128]{4,3,2,1,0:T(8,128)} %get-tuple-element.394) | copy-start | bytes 2359300 | tf_op jit(solution)/shard_map/while
  72.5 0.9 copy-start.4
  73.4 11.4 %collective-permute-start = (f32[1,6,16,16,128]{4,3,2,1,0:T(8,128)S(1)}, f32[1,6,16,16,128]{4,3,2,1,0:T(8,128)S(1)}, u32[]{:S(2)}, u32[]{:S(2)}) collective-permute-start(f32[1,6,16,16,128]{4,3,2,1,0:T(8,128)S(1)} %get-tuple-element.393), channel_id=1, source_target_pairs={{0,8},{8,16},{16,24},{24,0},{1,9},{9,17},{17,25},{25,1},{2,10},{10... | collective-permute-start | bytes 2359304 | tf_op jit(solution)/shard_map/while/body/eval_jaxpr/ppermute | solution.py:13
  73.7 11.2 %copy-start.3 = (f32[1,6,16,16,128]{4,3,2,1,0:T(8,128)S(1)}, f32[1,6,16,16,128]{4,3,2,1,0:T(8,128)}, u32[]{:S(2)}) copy-start(f32[1,6,16,16,128]{4,3,2,1,0:T(8,128)} %get-tuple-element.394) | copy-start | bytes 2359300 | tf_op jit(solution)/shard_map/while
  85.2 0.9 copy-start.4
  90.3 60.1 %copy-start.5 = (f32[6,16,16,128]{3,2,1,0:T(8,128)}, f32[6,16,16,128]{3,2,1,0:T(8,128)S(1)}, u32[]{:S(2)}) copy-start(f32[6,16,16,128]{3,2,1,0:T(8,128)S(1)} %get-tuple-element.272) | copy-start | bytes 2359300
  92.3 7.2 %collective-permute-start.6 = (f32[12,1,16,128]{3,2,1,0:T(8,128)S(1)}, f32[12,1,16,128]{3,2,1,0:T(8,128)S(1)}, u32[]{:S(2)}, u32[]{:S(2)}) collective-permute-start(f32[12,1,16,128]{3,2,1,0:T(8,128)S(1)} %get-tuple-element.278), channel_id=1, source_target_pairs={{0,2},{2,4},{4,6},{1,3},{3,5},{5,7},{8,10},{10,12},{12,14},{9,11},... | collective-permute-start | bytes 294920 | tf_op jit(solution)/shard_map/ppermute | solution.py:21
  95.6 54.7 %collective-permute-start.7 = (f32[12,1,16,128]{3,2,1,0:T(8,128)}, f32[12,1,16,128]{3,2,1,0:T(8,128)}, u32[]{:S(2)}, u32[]{:S(2)}) collective-permute-start(f32[12,1,16,128]{3,2,1,0:T(8,128)} %get-tuple-element.279), channel_id=1, source_target_pairs={{2,0},{4,2},{6,4},{3,1},{5,3},{7,5},{10,8},{12,10},{14,12},{11,9},... | collective-permute-start | bytes 294920 | tf_op jit(solution)/shard_map/ppermute | solution.py:24
  99.6 0.6 copy-start.9
  99.6 0.8 copy-start.14
  142.1 17.1 %all-to-all-start.1 = ((f32[4,6,16,128]{3,2,1,0:T(8,128)}), f32[4,6,16,128]{3,2,1,0:T(8,128)}, u32[]{:S(2)}, u32[]{:S(2)}) async-start(f32[4,6,16,128]{3,2,1,0:T(8,128)} %copy.51), calls=%async_computation.1 | async-start | bytes 393216 | tf_op jit(solution)/shard_map/all_to_all | solution.py:69
  149.4 0.9 copy-start.10
  152.0 47.3 %collective-permute-start.9 = (f32[12,18,1,128]{3,2,1,0:T(1,128)}, f32[12,18,1,128]{3,2,1,0:T(1,128)}, u32[]{:S(2)}, u32[]{:S(2)}) collective-permute-start(f32[12,18,1,128]{3,2,1,0:T(1,128)} %get-tuple-element.275), channel_id=1, source_target_pairs={{1,0},{3,2},{5,4},{7,6},{9,8},{11,10},{13,12},{15,14},{17,16},{19,... | collective-permute-start | bytes 331784 | tf_op jit(solution)/shard_map/ppermute | solution.py:24
  153.3 6.9 %copy-start.11 = (f32[12,1,16,128]{3,2,1,0:T(8,128)S(1)}, f32[12,1,16,128]{3,2,1,0:T(8,128)}, u32[]{:S(2)}) copy-start(f32[12,1,16,128]{3,2,1,0:T(8,128)} %copy-done.9) | copy-start | bytes 294916
  153.3 46.0 %collective-permute-start.8 = (f32[12,18,1,128]{3,2,1,0:T(1,128)}, f32[12,18,1,128]{3,2,1,0:T(1,128)}, u32[]{:S(2)}, u32[]{:S(2)}) collective-permute-start(f32[12,18,1,128]{3,2,1,0:T(1,128)} %get-tuple-element.274), channel_id=1, source_target_pairs={{0,1},{2,3},{4,5},{6,7},{8,9},{10,11},{12,13},{14,15},{16,17},{18,... | collective-permute-start | bytes 331784 | tf_op jit(solution)/shard_map/ppermute | solution.py:21
  160.9 11.6 %collective-permute-start.1 = (f32[1,6,16,16,128]{4,3,2,1,0:T(8,128)}, f32[1,6,16,16,128]{4,3,2,1,0:T(8,128)S(1)}, u32[]{:S(2)}, u32[]{:S(2)}) collective-permute-start(f32[1,6,16,16,128]{4,3,2,1,0:T(8,128)} %get-tuple-element.438), channel_id=1, source_target_pairs={{0,8},{8,16},{16,24},{24,0},{1,9},{9,17},{17,25},{25,1},{2,10},{10... | collective-permute-start | bytes 2359304 | tf_op jit(solution)/shard_map/while/body/eval_jaxpr/ppermute | solution.py:13
  173.6 11.7 %collective-permute-start.1 = (f32[1,6,16,16,128]{4,3,2,1,0:T(8,128)}, f32[1,6,16,16,128]{4,3,2,1,0:T(8,128)S(1)}, u32[]{:S(2)}, u32[]{:S(2)}) collective-permute-start(f32[1,6,16,16,128]{4,3,2,1,0:T(8,128)} %get-tuple-element.438), channel_id=1, source_target_pairs={{0,8},{8,16},{16,24},{24,0},{1,9},{9,17},{17,25},{25,1},{2,10},{10... | collective-permute-start | bytes 2359304 | tf_op jit(solution)/shard_map/while/body/eval_jaxpr/ppermute | solution.py:13
  186.5 11.7 %collective-permute-start.1 = (f32[1,6,16,16,128]{4,3,2,1,0:T(8,128)}, f32[1,6,16,16,128]{4,3,2,1,0:T(8,128)S(1)}, u32[]{:S(2)}, u32[]{:S(2)}) collective-permute-start(f32[1,6,16,16,128]{4,3,2,1,0:T(8,128)} %get-tuple-element.438), channel_id=1, source_target_pairs={{0,8},{8,16},{16,24},{24,0},{1,9},{9,17},{17,25},{25,1},{2,10},{10... | collective-permute-start | bytes 2359304 | tf_op jit(solution)/shard_map/while/body/eval_jaxpr/ppermute | solution.py:13
where the time goes:
time: 207 us; the launch traced here: 204 us
  waiting for transfers between devices  67.5 us (33%)
  local copies, waits for them, and re-layouts  42.4 us (20%)
  matrix products  36.1 us (17%)
  starting transfers between devices  34.9 us (17%)
  other arithmetic  21.1 us (10%)
    ppermute x6, waiting for transfers between devices, shifted(): return lax.ppermute(value, axis, pairs)  67.5 us
    dot_general x32, matrix products, one_row(): jnp.einsum('vjk,jkc->vc', row_values, onehot, precision=lax.Precision.HIG...  31.3 us
    eq x32, local copies, waits for them, and re-layouts, one_row(): onehot = (row_targets[..., None] == columns).astype(jnp.float32)  22 us
    ppermute x4, starting transfers between devices, with_halo(): lax.ppermute(lax.slice_in_dim(block, block.shape[dim] - width, None, axis...  17.9 us
    ppermute x4, starting transfers between devices, with_halo(): lax.ppermute(lax.slice_in_dim(block, 0, width, axis=dim), axis, backward)  8.82 us
    all_to_all x2, starting transfers between devices, sender_inflow(): lax.all_to_all(blocks, 'inst', split_axis=0, concat_axis=0, tiled=True)  8.11 us
    mul x2, other arithmetic, operator(): flux = axial_speed[None] * plain  5.57 us
    slice x4, local copies, waits for them, and re-layouts, operator(): t_low = jnp.roll(plain, 1, axis=3)  5.57 us
  transfers between devices with their start and end apart: 16, of which 6 were waited for; matrix products, arithmetic and copies ran while one was open for 40% of the time, Pallas kernels for 0%

commit v1 on v0

v1 whole, which is shorter than its diff:
```python
import functools
import math

import jax
import jax.numpy as jnp
from jax import lax
from jax.experimental import pallas as pl
from jax.experimental.pallas import tpu as pltpu
from jax.sharding import PartitionSpec as P

omega_scale = 0.5
pseudo_step = 0.5
MESH = pl.DeviceIdType.MESH


def coefficients(count):
    once = [0.0] + [
        omega_scale * 0.5 * (-1.0) ** k * math.cos(math.pi * k / count) / math.sin(math.pi * k / count)
        for k in range(1, count)
    ]
    twice = [sum(once[i] * once[(k - i) % count] for i in range(count)) for k in range(count)]
    return once, twice


def chunk_list(planes):
    chunks = [(planes - 1, 1), (0, 1)]
    start = 1
    while start < planes - 1:
        size = min(2, planes - 1 - start)
        chunks.append((start, size))
        start += size
    return chunks


def kernel(
    count, streams, rads, nvars, planes, rows, width,
    u, axial, cross, viscosity, coupling, targets, shares, out,
    up, axp, xb, cb, f, ur, urs, fr, frs, wv, bs, br, ds, dr, gathered,
    local_sem, x_send, x_recv, c_send, c_recv, uz_send, uz_recv, fz_send, fz_recv,
    a_send, a_recv, ur_send, ur_recv, fr_send, fr_recv, b_send, b_recv, d_send, d_recv,
):
    chips = count // 2
    chunks = chunk_list(planes)
    once, twice = coefficients(count)
    half_step = 0.5 * pseudo_step
    vpad = fr.shape[2]
    me = lax.axis_index("inst")
    z = lax.axis_index("stream")
    r = lax.axis_index("rad")
    chip, core = me // 2, lax.rem(me, 2)
    peer = me + 1 - 2 * core
    has_zlo, has_zhi = z > 0, z < streams - 1
    has_rlo, has_rhi = r > 0, r < rads - 1
    face = z == streams // 2 - 1
    stator = z == streams // 2

    def rows_of(s, n=1, shift=0):
        return pl.ds((s + shift) * rows, n * rows)

    def row_at(s, shift=0):
        return pl.ds(pl.multiple_of((s + shift) * rows, rows), rows)

    def x_copy(d, j):
        s, n = chunks[j]
        return pltpu.make_async_remote_copy(
            src_ref=u.at[:, rows_of(s, n), :], dst_ref=xb.at[d - 1, :, rows_of(s, n), :],
            send_sem=x_send.at[d - 1, j], recv_sem=x_recv.at[d - 1, j],
            device_id={"inst": lax.rem(chip + d, chips) * 2 + core}, device_id_type=MESH)

    def c_copy(d, j):
        s, n = chunks[j]
        source = u if d == 0 else xb.at[d - 1]
        return pltpu.make_async_remote_copy(
            src_ref=source.at[:, rows_of(s, n), :], dst_ref=cb.at[d, :, rows_of(s, n), :],
            send_sem=c_send.at[d, j], recv_sem=c_recv.at[d, j],
            device_id={"inst": peer}, device_id_type=MESH)

    def z_copy(to_high, source, shift, field, send, recv):
        own = rows_of(planes - 1 if to_high else 0, 1, shift)
        landing = rows_of(0 if to_high else planes + 1)
        return pltpu.make_async_remote_copy(
            src_ref=source.at[:, own, :], dst_ref=field.at[:, landing, :],
            send_sem=send.at[1 - to_high], recv_sem=recv.at[1 - to_high],
            device_id={"stream": z + 1 if to_high else z - 1}, device_id_type=MESH)

    def uz_copy(to_high):
        return z_copy(to_high, u, 0, up, uz_send, uz_recv)

    def fz_copy(to_high):
        return z_copy(to_high, f, 1, f, fz_send, fz_recv)

    def a_copy():
        return pltpu.make_async_remote_copy(
            src_ref=axial.at[rows_of(planes - 1), :], dst_ref=axp.at[rows_of(0), :],
            send_sem=a_send.at[0], recv_sem=a_recv.at[0],
            device_id={"stream": z + 1}, device_id_type=MESH)

    def ur_copy(to_high):
        side = 1 - to_high
        return pltpu.make_async_remote_copy(
            src_ref=urs.at[side], dst_ref=ur.at[side],
            send_sem=ur_send.at[side], recv_sem=ur_recv.at[side],
            device_id={"rad": r + 1 if to_high else r - 1}, device_id_type=MESH)

    def fr_copy(to_high, j):
        s, n = chunks[j]
        side = 1 - to_high
        return pltpu.make_async_remote_copy(
            src_ref=frs.at[side, pl.ds(s, n)], dst_ref=fr.at[side, pl.ds(s, n)],
            send_sem=fr_send.at[side, j], recv_sem=fr_recv.at[side, j],
            device_id={"rad": r + 1 if to_high else r - 1}, device_id_type=MESH)

    def face_copy(source, landing, send, recv, m, slot):
        return pltpu.make_async_remote_copy(
            src_ref=source.at[m], dst_ref=landing.at[slot],
            send_sem=send.at[m], recv_sem=recv.at[slot],
            device_id={"inst": m, "stream": z + 1}, device_id_type=MESH)

    def local_copies():
        return [
            pltpu.make_async_copy(u, up.at[:, rows_of(0, planes, 1), :], local_sem.at[0]),
            pltpu.make_async_copy(axial, axp.at[rows_of(0, planes, 1), :], local_sem.at[1]),
        ]

    for copy in local_copies():
        copy.start()

    barrier = pltpu.get_barrier_semaphore()

    def greet(**device):
        pl.semaphore_signal(barrier, inc=1, device_id=device, device_id_type=MESH)

    greet(inst=peer)
    for d in range(1, chips):
        greet(inst=lax.rem(chip + d, chips) * 2 + core)
    pl.when(has_zlo)(lambda: greet(stream=z - 1))
    pl.when(has_zhi)(lambda: greet(stream=z + 1))
    pl.when(has_rlo)(lambda: greet(rad=r - 1))
    pl.when(has_rhi)(lambda: greet(rad=r + 1))
    for d in range(1, count):
        other = lax.rem(me + d, count)
        pl.when(face)(functools.partial(greet, inst=other, stream=z + 1))
        pl.when(stator)(functools.partial(greet, inst=other, stream=z - 1))
    one = lambda flag: flag.astype(jnp.int32)
    expected = chips + one(has_zlo) + one(has_zhi) + one(has_rlo) + one(has_rhi)
    expected = expected + (count - 1) * (one(face) + one(stator))

    plane_zero = jnp.zeros((rows, width), jnp.float32)

    def zero_plane(field, p):
        for v in range(nvars):
            field[v, rows_of(p), :] = plane_zero

    @pl.when(jnp.logical_not(has_zlo))
    def _():
        zero_plane(up, 0)
        zero_plane(f, 0)

    @pl.when(jnp.logical_not(has_zhi))
    def _():
        zero_plane(up, planes + 1)
        zero_plane(f, planes + 1)

    no_axial = jnp.logical_or(jnp.logical_not(has_zlo), stator)

    @pl.when(no_axial)
    def _():
        axp[rows_of(0), :] = plane_zero

    @pl.when(jnp.logical_not(has_rlo))
    def _():
        ur[0] = jnp.zeros(ur.shape[1:], jnp.float32)
        fr[0] = jnp.zeros(fr.shape[1:], jnp.float32)

    @pl.when(jnp.logical_not(has_rhi))
    def _():
        ur[1] = jnp.zeros(ur.shape[1:], jnp.float32)
        fr[1] = jnp.zeros(fr.shape[1:], jnp.float32)

    urs[...] = jnp.zeros(urs.shape, jnp.float32)
    frs[...] = jnp.zeros(frs.shape, jnp.float32)
    wv[...] = jnp.zeros(wv.shape, jnp.float32)

    pl.semaphore_wait(barrier, expected)

    for j in range(len(chunks)):
        for d in range(1, chips):
            x_copy(d, j).start()
    for j in range(len(chunks)):
        c_copy(0, j).start()
    pl.when(has_zhi)(lambda: uz_copy(1).start())
    pl.when(has_zlo)(lambda: uz_copy(0).start())
    sends_axial = jnp.logical_and(has_zhi, jnp.logical_not(face))
    pl.when(sends_axial)(lambda: a_copy().start())

    for copy in local_copies():
        copy.wait()

    @pl.loop(0, planes)
    def _(s):
        base = (s + 1) * rows
        for v in range(nvars):
            urs[0, s, v:v + 1, :] = up[v, pl.ds(base + rows - 1, 1), :]
            urs[1, s, v:v + 1, :] = up[v, pl.ds(base, 1), :]

    pl.when(has_rhi)(lambda: ur_copy(1).start())
    pl.when(has_rlo)(lambda: ur_copy(0).start())

    def scatter(result):
        span = min(count, 4) * width

        @pl.loop(0, rows)
        def _(row):
            flux = wv[pl.ds(pl.multiple_of(row * vpad, vpad), vpad), :]
            share = shares[pl.ds(row, 1), :]
            parts = []
            for value in (flux * share, flux * (1.0 - share)):
                high = value.astype(jnp.bfloat16).astype(jnp.float32)
                rest = value - high
                middle = rest.astype(jnp.bfloat16).astype(jnp.float32)
                stack = jnp.concatenate([high, middle, rest - middle], axis=0)
                parts.append(stack.astype(jnp.bfloat16))
            slots = lax.broadcasted_iota(jnp.int32, (span, width), 0)
            for start in range(0, count * width, span):
                total = jnp.zeros((3 * vpad, span), jnp.float32)
                for k in range(2):
                    target = targets[pl.ds(k * rows + row, 1), :]
                    hit = (slots + start == target).astype(jnp.float32).astype(jnp.bfloat16)
                    total = total + lax.dot_general(
                        parts[k], hit, (((1,), (1,)), ((), ())),
                        preferred_element_type=jnp.float32)
                total = total[:vpad] + total[vpad:2 * vpad] + total[2 * vpad:]
                for i in range(span // width):
                    result[start // width + i, pl.ds(pl.multiple_of(row * vpad, vpad), vpad), :] = (
                        total[:, i * width:(i + 1) * width])

    @pl.when(face)
    def _():
        speed = axp[rows_of(planes), :]
        for v in range(nvars):
            wv[pl.ds(v, rows, stride=vpad), :] = speed * up[v, rows_of(planes), :]
        scatter(bs)
        for m in range(count):
            face_copy(bs, br, b_send, b_recv, m, me).start()

    row_index = lax.broadcasted_iota(jnp.int32, (rows, width), 0)
    first_row, last_row = row_index == 0, row_index == rows - 1

    def operator(s, field, halo):
        a = cross[0, row_at(s), :]
        b = cross[1, row_at(s), :]
        nu = viscosity[row_at(s), :]
        ap, am = jnp.maximum(a, 0.0), jnp.minimum(a, 0.0)
        bp, bm = jnp.maximum(b, 0.0), jnp.minimum(b, 0.0)
        centre = axp[row_at(s, 1), :] + (ap - am) + (bp - bm) + 6.0 * nu
        s_low = axp[row_at(s), :] + nu
        r_low, r_high, t_low, t_high = ap + nu, nu - am, bp + nu, nu - bm
        here = [field[v, row_at(s, 1), :] for v in range(nvars)]
        results = []
        for v in range(nvars):
            value = here[v]
            below = jnp.where(first_row, halo[0, s, v:v + 1, :], pltpu.roll(value, 1, 0))
            above = jnp.where(last_row, halo[1, s, v:v + 1, :], pltpu.roll(value, rows - 1, 0))
            total = centre * value
            total = total - s_low * field[v, row_at(s), :] - nu * field[v, row_at(s, 2), :]
            total = total - r_low * below - r_high * above
            total = total - t_low * pltpu.roll(value, 1, 1) - t_high * pltpu.roll(value, width - 1, 1)
            for w in range(nvars):
                total = total + coupling[v, w] * here[w]
            results.append(total)
        return here, results

    pl.when(has_zlo)(lambda: uz_copy(1).wait_recv())
    pl.when(has_zhi)(lambda: uz_copy(0).wait_recv())
    pl.when(jnp.logical_not(no_axial))(lambda: a_copy().wait_recv())
    pl.when(has_rlo)(lambda: ur_copy(1).wait_recv())
    pl.when(has_rhi)(lambda: ur_copy(0).wait_recv())

    @pl.loop(0, planes)
    def _(s):
        here, results = operator(s, up, ur)
        for v in range(nvars):
            f[v, row_at(s, 1), :] = here[v] - half_step * results[v]

    def gather(landing, recv):
        for n in range(count):
            face_copy(landing, landing, recv, recv, 0, n).wait_recv()
        total = landing[0]
        for n in range(1, count):
            total = total + landing[n]
        gathered[...] = total

    @pl.when(stator)
    def _():
        gather(br, b_recv)
        for v in range(nvars):
            f[v, rows_of(0, 1, 1), :] += half_step * gathered[pl.ds(v, rows, stride=vpad), :]

    pairs = [(once[k], once[k] - half_step * twice[k]) for k in range(count)]
    zero_step = lax.convert_element_type(core, jnp.int32) == 0
    terms = []
    for d in range(1, chips):
        terms.append((xb, d - 1, pairs[2 * d]))
    for d in range(chips):
        low, high = pairs[(2 * d - 1) % count], pairs[(2 * d + 1) % count]
        terms.append((cb, d, tuple(jnp.where(zero_step, jnp.float32(lo), jnp.float32(hi)) for lo, hi in zip(low, high))))

    def process(j):
        s0, n = chunks[j]
        for d in range(chips):
            c_copy(d, j).wait_recv()

        for s in range(s0, s0 + n):
            for v in range(nvars):
                own = up[v, rows_of(s, 1, 1), :]
                spectral = pairs[0][0] * own if pairs[0][0] else None
                combined = pairs[0][1] * own
                for buffer, slot, (c, g) in terms:
                    value = buffer[slot, v, rows_of(s), :]
                    spectral = c * value if spectral is None else spectral + c * value
                    combined = combined + g * value
                new = f[v, rows_of(s, 1, 1), :] - pseudo_step * spectral
                f[v, rows_of(s, 1, 1), :] = new
                out[v, rows_of(s), :] = own - pseudo_step * combined
                frs[0, s, v:v + 1, :] = new[rows - 1:rows]
                frs[1, s, v:v + 1, :] = new[0:1]
                if s == planes - 1:
                    wv[pl.ds(v, rows, stride=vpad), :] = axp[rows_of(planes), :] * (new + half_step * spectral)
        pl.when(has_rhi)(lambda: fr_copy(1, j).start())
        pl.when(has_rlo)(lambda: fr_copy(0, j).start())
        if s0 == planes - 1:
            pl.when(has_zhi)(lambda: fz_copy(1).start())

            @pl.when(face)
            def _():
                scatter(ds)
                for m in range(count):
                    total = -ds[m]
                    for k in range(1, count):
                        total = total + (half_step * once[k]) * bs[(m - k) % count]
                    ds[m] = total
                for m in range(count):
                    face_copy(ds, dr, d_send, d_recv, m, me).start()
        if s0 == 0:
            pl.when(has_zlo)(lambda: fz_copy(0).start())

    def finish(s, n):
        @pl.loop(s, s + n)
        def _(s):
            _, results = operator(s, f, fr)
            for v in range(nvars):
                out[v, row_at(s), :] -= pseudo_step * results[v]

    done = {0, planes - 1}
    ready = set()

    def finals(j):
        s0, n = chunks[j]
        pl.when(has_rlo)(lambda: fr_copy(1, j).wait_recv())
        pl.when(has_rhi)(lambda: fr_copy(0, j).wait_recv())
        ready.update(range(s0, s0 + n))
        able = [s for s in range(1, planes - 1)
                if s not in done and {s - 1, s, s + 1} <= ready]
        if able:
            done.update(able)
            finish(able[0], len(able))
        if j == len(chunks) - 2:
            pl.when(has_zlo)(lambda: fz_copy(1).wait_recv())
            pl.when(has_zhi)(lambda: fz_copy(0).wait_recv())
            finish(0, 1)

            @pl.when(stator)
            def _():
                gather(dr, d_recv)
                for v in range(nvars):
                    out[v, rows_of(0), :] -= pseudo_step * gathered[pl.ds(v, rows, stride=vpad), :]
        if j == len(chunks) - 1:
            finish(planes - 1, 1)

    steps = len(chunks)
    for j in range(steps + 2):
        if j < steps:
            for d in range(1, chips):
                x_copy(d, j).wait_recv()
                c_copy(d, j).start()
        if 1 <= j <= steps:
            process(j - 1)
        if 2 <= j:
            finals(j - 2)

    for j in range(steps):
        for d in range(1, chips):
            x_copy(d, j).wait_send()
        for d in range(chips):
            c_copy(d, j).wait_send()
    @pl.when(has_rhi)
    def _():
        ur_copy(1).wait_send()
        for j in range(steps):
            fr_copy(1, j).wait_send()

    @pl.when(has_rlo)
    def _():
        ur_copy(0).wait_send()
        for j in range(steps):
            fr_copy(0, j).wait_send()

    @pl.when(has_zhi)
    def _():
        uz_copy(1).wait_send()
        fz_copy(1).wait_send()

    @pl.when(has_zlo)
    def _():
        uz_copy(0).wait_send()
        fz_copy(0).wait_send()

    pl.when(sends_axial)(lambda: a_copy().wait_send())

    @pl.when(face)
    def _():
        for m in range(count):
            face_copy(bs, br, b_send, b_recv, m, me).wait_send()
            face_copy(ds, dr, d_send, d_recv, m, me).wait_send()


def body(state, axial_speed, cross_speed, viscosity, coupling, targets, shares):
    count, streams, rads = (lax.axis_size(name) for name in ("inst", "stream", "rad"))
    _, nvars, planes, rows, width = state.shape
    chips, chunks = count // 2, len(chunk_list(planes))
    vpad = -(-nvars // 8) * 8
    cells = planes * rows
    vmem = pl.BlockSpec(memory_space=pltpu.VMEM)
    dma = pltpu.SemaphoreType.DMA
    buf = lambda *shape: pltpu.VMEM(shape, jnp.float32)
    result = pl.pallas_call(
        functools.partial(kernel, count, streams, rads, nvars, planes, rows, width),
        out_shape=jax.ShapeDtypeStruct((nvars, cells, width), jnp.float32),
        in_specs=[pl.BlockSpec(memory_space=pl.ANY), vmem, vmem, vmem,
                  pl.BlockSpec(memory_space=pltpu.SMEM), vmem, vmem],
        out_specs=vmem,
        scratch_shapes=[
            buf(nvars, cells + 2 * rows, width), buf(cells + rows, width),
            buf(chips - 1, nvars, cells, width), buf(chips, nvars, cells, width),
            buf(nvars, cells + 2 * rows, width),
            buf(2, planes, vpad, width), buf(2, planes, vpad, width),
            buf(2, planes, vpad, width), buf(2, planes, vpad, width),
            buf(rows * vpad, width),
            buf(count, rows * vpad, width), buf(count, rows * vpad, width),
            buf(count, rows * vpad, width), buf(count, rows * vpad, width),
            buf(rows * vpad, width),
            dma((2,)), dma((chips - 1, chunks)), dma((chips - 1, chunks)),
            dma((chips, chunks)), dma((chips, chunks)),
            dma((2,)), dma((2,)), dma((2,)), dma((2,)), dma((1,)), dma((1,)),
            dma((2,)), dma((2,)), dma((2, chunks)), dma((2, chunks)),
            dma((count,)), dma((count,)), dma((count,)), dma((count,)),
        ],
        compiler_params=pltpu.CompilerParams(
            collective_id=0, has_side_effects=True, vmem_limit_bytes=48 * 1024 * 1024),
    )(
        state.reshape(nvars, cells, width), axial_speed.reshape(cells, width),
        cross_speed.reshape(2, cells, width), viscosity.reshape(cells, width), coupling,
        jnp.transpose(targets[0], (2, 0, 1)).reshape(2 * rows, width), shares[0],
    )
    return result.reshape(state.shape)


def solution(mesh):
    in_specs = (
        P("inst", None, "stream", "rad", None),
        P("stream", "rad", None),
        P(None, "stream", "rad", None),
        P("stream", "rad", None),
        P(),
        P("inst", "rad", None, None),
        P("inst", "rad", None),
    )
    out_specs = P("inst", None, "stream", "rad", None)
    return jax.shard_map(body, mesh=mesh, in_specs=in_specs, out_specs=out_specs, check_vma=False)
```

time: 207 us -> 38.8 us (0.19); the launches traced: 204 us -> 38.5 us
  waiting for transfers between devices: 67.5 us -> 0 us
  local copies, waits for them, and re-layouts: 42.4 us -> 5.52 us
  matrix products: 36.1 us -> 0 us
  starting transfers between devices: 34.9 us -> 0 us
  Pallas kernels: 0 us -> 33 us
  other arithmetic: 21.1 us -> 0 us
    ppermute x14 -> x0, waiting for transfers between devices: 67.5 us -> none  [the longest x6 67.5 us: shifted(): return lax.ppermute(value, axis, pairs)]
    dot_general x34 -> x0, matrix products: 36.1 us -> none  [the longest x32 31.3 us: one_row(): jnp.einsum('vjk,jkc->vc', row_values, onehot, precision=lax.Precision.HIG...]
    pallas_call x0 -> x1, Pallas kernels: none -> 33 us  [body(): pl.pallas_call(functools.partial(kernel, count, streams, rads, nvars, pla...]
    ppermute x14 -> x0, starting transfers between devices: 26.8 us -> none  [the longest x4 17.9 us: with_halo(): lax.ppermute(lax.slice_in_dim(block, block.shape[dim] - width, None, axis...]
    eq x32 -> x0, local copies, waits for them, and re-layouts: 22 us -> none  [one_row(): onehot = (row_targets[..., None] == columns).astype(jnp.float32)]
    all_to_all x2 -> x0, starting transfers between devices: 8.11 us -> none  [sender_inflow(): lax.all_to_all(blocks, 'inst', split_axis=0, concat_axis=0, tiled=True)]
    slice x6 -> x0, local copies, waits for them, and re-layouts: 7.4 us -> none  [the longest x4 5.57 us: operator(): t_low = jnp.roll(plain, 1, axis=3)]
    mul x5 -> x0, other arithmetic: 6.92 us -> none  [the longest x2 5.57 us: operator(): flux = axial_speed[None] * plain]
  transfers between devices with their start and end apart: 16 -> 0, of which waited for: 6 -> 0; matrix products, arithmetic and copies ran while one was open for 40% -> 0% of each run, Pallas kernels for 0% -> 0%
where the time goes in v1:
time: 38.8 us; the launch traced here: 38.5 us
  Pallas kernels  33 us (85%)
  local copies, waits for them, and re-layouts  5.52 us (14%)
    pallas_call x1, Pallas kernels, body(): pl.pallas_call(functools.partial(kernel, count, streams, rads, nvars, pla...  33 us
    unnamed x13, local copies, waits for them, and re-layouts  4.78 us

profile of v1, /device:TPU:16, one launch (start us, length us, event | category | flops | bytes accessed | tf_op | source)
XLA Modules:
  0.0 38.5 jit_solution(864455433753131595)
XLA Ops:
  0.0 0.0 copy-start.4
  0.0 0.0 copy-start.5
  0.0 0.7 %copy.8 = s32[2,16,128]{2,1,0:T(8,128)S(1)} copy(s32[2,16,128]{2,0,1:T(2,128)} %bitcast.17) | data formatting | bytes 32768 | tf_op jit(solution)/shard_map/transpose | solution.py:463
  0.8 0.0 copy-done.4
  0.8 0.0 copy-done.5
  0.8 0.0 copy-start
  0.8 1.1 %copy-done = f32[1,6,16,16,128]{4,3,2,1,0:T(8,128)S(1)} copy-done((f32[1,6,16,16,128]{4,3,2,1,0:T(8,128)S(1)}, f32[1,6,16,16,128]{4,3,2,1,0:T(8,128)}, u32[]{:S(2)}) %copy-start) | copy-done | bytes 786456
  1.9 0.0 copy-start.1
  1.9 0.9 %copy-done.1 = f32[2,16,16,128]{3,2,1,0:T(8,128)S(1)} copy-done((f32[2,16,16,128]{3,2,1,0:T(8,128)S(1)}, f32[2,16,16,128]{3,2,1,0:T(8,128)}, u32[]{:S(2)}) %copy-start.1) | copy-done | bytes 262168
  2.8 0.0 copy-start.2
  2.8 0.9 %copy-done.2 = f32[16,16,128]{2,1,0:T(8,128)S(1)} copy-done((f32[16,16,128]{2,1,0:T(8,128)S(1)}, f32[16,16,128]{2,1,0:T(8,128)}, u32[]{:S(2)}) %copy-start.2) | copy-done | bytes 131096
  3.7 0.0 copy-start.3
  3.7 0.9 %copy-done.3 = f32[16,16,128]{2,1,0:T(8,128)S(1)} copy-done((f32[16,16,128]{2,1,0:T(8,128)S(1)}, f32[16,16,128]{2,1,0:T(8,128)}, u32[]{:S(2)}) %copy-start.3) | copy-done | bytes 131096
  4.7 33.0 %shard_map.73 = f32[6,256,128]{2,1,0:T(8,128)S(1)} custom-call(f32[6,256,128]{2,1,0:T(8,128)S(1)} %bitcast.11, f32[256,128]{1,0:T(8,128)S(1)} %bitcast.13, f32[2,256,128]{2,1,0:T(8,128)S(1)} %bitcast.12, f32[256,128]{1,0:T(8,128)S(1)} %bitcast.14, f32[6,6]{1,0:T(8,128)S(1)} %copy-done.5, s32[32,128]{1,0:T(8,128)S(1)} %bitcast.15, f32[16,128]{1,0:T(8,128)S(1)} %bitcast.16), custom_call_target="tpu_custom_call" | custom-call | tf_op jit(solution)/shard_map/pallas_call | solution.py:436
  37.6 0.9 %copy.10 = f32[1,6,16,16,128]{4,3,2,1,0:T(8,128)} copy(f32[1,6,16,16,128]{4,3,2,1,0:T(8,128)S(1)} %bitcast.10) | data formatting | bytes 1572864
Async XLA Ops:
  0.0 0.8 %copy-start.4 = (f32[1,16,128]{2,1,0:T(8,128)S(1)}, f32[1,16,128]{2,1,0:T(8,128)}, u32[]{:S(2)}) copy-start(f32[1,16,128]{2,1,0:T(8,128)} %param.13) | copy-start | bytes 24580
  0.0 0.8 %copy-start.5 = (f32[6,6]{1,0:T(8,128)S(1)}, f32[6,6]{1,0:T(8,128)}, u32[]{:S(2)}) copy-start(f32[6,6]{1,0:T(8,128)} %coupling.1) | copy-start | bytes 436
  0.8 1.1 %copy-start = (f32[1,6,16,16,128]{4,3,2,1,0:T(8,128)S(1)}, f32[1,6,16,16,128]{4,3,2,1,0:T(8,128)}, u32[]{:S(2)}) copy-start(f32[1,6,16,16,128]{4,3,2,1,0:T(8,128)} %param.7) | copy-start | bytes 2359300
  1.9 0.9 %copy-start.1 = (f32[2,16,16,128]{3,2,1,0:T(8,128)S(1)}, f32[2,16,16,128]{3,2,1,0:T(8,128)}, u32[]{:S(2)}) copy-start(f32[2,16,16,128]{3,2,1,0:T(8,128)} %param.9) | copy-start | bytes 786436
  2.8 0.9 %copy-start.2 = (f32[16,16,128]{2,1,0:T(8,128)S(1)}, f32[16,16,128]{2,1,0:T(8,128)}, u32[]{:S(2)}) copy-start(f32[16,16,128]{2,1,0:T(8,128)} %param.8) | copy-start | bytes 393220
  3.7 0.9 %copy-start.3 = (f32[16,16,128]{2,1,0:T(8,128)S(1)}, f32[16,16,128]{2,1,0:T(8,128)}, u32[]{:S(2)}) copy-start(f32[16,16,128]{2,1,0:T(8,128)} %param.10) | copy-start | bytes 393220

commit v2 on v1

--- a/solution.py
+++ b/solution.py
@@ -23,19 +23,20 @@
 
 
 def chunk_list(planes):
-    chunks = [(planes - 1, 1), (0, 1)]
+    chunks = [(planes - 1, 1)]
     start = 1
     while start < planes - 1:
         size = min(2, planes - 1 - start)
         chunks.append((start, size))
         start += size
+    chunks.insert(len(chunks) - 2, (0, 1))
     return chunks
 
 
 def kernel(
     count, streams, rads, nvars, planes, rows, width,
-    u, axial, cross, viscosity, coupling, targets, shares, out,
-    up, axp, xb, cb, f, ur, urs, fr, frs, wv, bs, br, ds, dr, gathered,
+    u, axial, cross_in, viscosity_in, coupling, targets_in, shares_in, out,
+    up, axp, cross, viscosity, targets, shares, wide, xb, cb, f, ur, urs, fr, frs, wv, bs, br, ds, dr,
     local_sem, x_send, x_recv, c_send, c_recv, uz_send, uz_recv, fz_send, fz_recv,
     a_send, a_recv, ur_send, ur_recv, fr_send, fr_recv, b_send, b_recv, d_send, d_recv,
 ):
@@ -116,11 +117,16 @@
             send_sem=send.at[m], recv_sem=recv.at[slot],
             device_id={"inst": m, "stream": z + 1}, device_id_type=MESH)
 
-    def local_copies():
-        return [
-            pltpu.make_async_copy(u, up.at[:, rows_of(0, planes, 1), :], local_sem.at[0]),
-            pltpu.make_async_copy(axial, axp.at[rows_of(0, planes, 1), :], local_sem.at[1]),
+    def local_copies(first=0, last=6):
+        pairs = [
+            (u, up.at[:, rows_of(0, planes, 1), :]),
+            (axial, axp.at[rows_of(0, planes, 1), :]),
+            (targets_in, targets),
+            (shares_in, shares),
+            (viscosity_in, viscosity),
+            (cross_in, cross),
         ]
+        return [pltpu.make_async_copy(*pairs[i], local_sem.at[i]) for i in range(first, last)]
 
     for copy in local_copies():
         copy.start()
@@ -183,7 +189,8 @@
 
     pl.semaphore_wait(barrier, expected)
 
-    for j in range(len(chunks)):
+    early = min(5, len(chunks))
+    for j in range(early):
         for d in range(1, chips):
             x_copy(d, j).start()
     for j in range(len(chunks)):
@@ -193,7 +200,7 @@
     sends_axial = jnp.logical_and(has_zhi, jnp.logical_not(face))
     pl.when(sends_axial)(lambda: a_copy().start())
 
-    for copy in local_copies():
+    for copy in local_copies(0, 4):
         copy.wait()
 
     @pl.loop(0, planes)
@@ -231,8 +238,12 @@
                         preferred_element_type=jnp.float32)
                 total = total[:vpad] + total[vpad:2 * vpad] + total[2 * vpad:]
                 for i in range(span // width):
-                    result[start // width + i, pl.ds(pl.multiple_of(row * vpad, vpad), vpad), :] = (
+                    wide[start // width + i, pl.ds(pl.multiple_of(row * vpad, vpad), vpad), :] = (
                         total[:, i * width:(i + 1) * width])
+
+        for m in range(count):
+            for v in range(nvars):
+                result[m, v] = wide[m, pl.ds(v, rows, stride=vpad), :]
 
     @pl.when(face)
     def _():
@@ -270,6 +281,8 @@
             results.append(total)
         return here, results
 
+    for copy in local_copies(4):
+        copy.wait()
     pl.when(has_zlo)(lambda: uz_copy(1).wait_recv())
     pl.when(has_zhi)(lambda: uz_copy(0).wait_recv())
     pl.when(jnp.logical_not(no_axial))(lambda: a_copy().wait_recv())
@@ -285,16 +298,7 @@
     def gather(landing, recv):
         for n in range(count):
             face_copy(landing, landing, recv, recv, 0, n).wait_recv()
-        total = landing[0]
-        for n in range(1, count):
-            total = total + landing[n]
-        gathered[...] = total
-
-    @pl.when(stator)
-    def _():
-        gather(br, b_recv)
-        for v in range(nvars):
-            f[v, rows_of(0, 1, 1), :] += half_step * gathered[pl.ds(v, rows, stride=vpad), :]
+        return [sum((landing[n, v] for n in range(1, count)), landing[0, v]) for v in range(nvars)]
 
     pairs = [(once[k], once[k] - half_step * twice[k]) for k in range(count)]
     zero_step = lax.convert_element_type(core, jnp.int32) == 0
@@ -309,6 +313,11 @@
         s0, n = chunks[j]
         for d in range(chips):
             c_copy(d, j).wait_recv()
+        if s0 == 0:
+            @pl.when(stator)
+            def _():
+                for v, inflow in enumerate(gather(br, b_recv)):
+                    f[v, rows_of(0, 1, 1), :] += half_step * inflow
 
         for s in range(s0, s0 + n):
             for v in range(nvars):
@@ -366,16 +375,15 @@
             finish(able[0], len(able))
         if j == len(chunks) - 2:
             pl.when(has_zlo)(lambda: fz_copy(1).wait_recv())
+            finish(0, 1)
+        if j == len(chunks) - 1:
             pl.when(has_zhi)(lambda: fz_copy(0).wait_recv())
-            finish(0, 1)
+            finish(planes - 1, 1)
 
             @pl.when(stator)
             def _():
-                gather(dr, d_recv)
-                for v in range(nvars):
-                    out[v, rows_of(0), :] -= pseudo_step * gathered[pl.ds(v, rows, stride=vpad), :]
-        if j == len(chunks) - 1:
-            finish(planes - 1, 1)
+                for v, inflow in enumerate(gather(dr, d_recv)):
+                    out[v, rows_of(0), :] -= pseudo_step * inflow
 
     steps = len(chunks)
     for j in range(steps + 2):
@@ -385,6 +393,10 @@
                 c_copy(d, j).start()
         if 1 <= j <= steps:
             process(j - 1)
+        if j == 1:
+            for later in range(early, steps):
+                for d in range(1, chips):
+                    x_copy(d, later).start()
         if 2 <= j:
             finals(j - 2)
 
@@ -431,32 +443,34 @@
     vpad = -(-nvars // 8) * 8
     cells = planes * rows
     vmem = pl.BlockSpec(memory_space=pltpu.VMEM)
+    hbm = pl.BlockSpec(memory_space=pltpu.HBM)
     dma = pltpu.SemaphoreType.DMA
     buf = lambda *shape: pltpu.VMEM(shape, jnp.float32)
     result = pl.pallas_call(
         functools.partial(kernel, count, streams, rads, nvars, planes, rows, width),
         out_shape=jax.ShapeDtypeStruct((nvars, cells, width), jnp.float32),
-        in_specs=[pl.BlockSpec(memory_space=pl.ANY), vmem, vmem, vmem,
-                  pl.BlockSpec(memory_space=pltpu.SMEM), vmem, vmem],
+        in_specs=[hbm, hbm, hbm, hbm, pl.BlockSpec(memory_space=pltpu.SMEM), hbm, hbm],
         out_specs=vmem,
         scratch_shapes=[
             buf(nvars, cells + 2 * rows, width), buf(cells + rows, width),
+            buf(2, cells, width), buf(cells, width),
+            pltpu.VMEM((2 * rows, width), jnp.int32), buf(rows, width),
+            buf(count, rows * vpad, width),
             buf(chips - 1, nvars, cells, width), buf(chips, nvars, cells, width),
             buf(nvars, cells + 2 * rows, width),
             buf(2, planes, vpad, width), buf(2, planes, vpad, width),
             buf(2, planes, vpad, width), buf(2, planes, vpad, width),
             buf(rows * vpad, width),
-            buf(count, rows * vpad, width), buf(count, rows * vpad, width),
-            buf(count, rows * vpad, width), buf(count, rows * vpad, width),
-            buf(rows * vpad, width),
-            dma((2,)), dma((chips - 1, chunks)), dma((chips - 1, chunks)),
+            buf(count, nvars, rows, width), buf(count, nvars, rows, width),
+            buf(count, nvars, rows, width), buf(count, nvars, rows, width),
+            dma((6,)), dma((chips - 1, chunks)), dma((chips - 1, chunks)),
             dma((chips, chunks)), dma((chips, chunks)),
             dma((2,)), dma((2,)), dma((2,)), dma((2,)), dma((1,)), dma((1,)),
             dma((2,)), dma((2,)), dma((2, chunks)), dma((2, chunks)),
             dma((count,)), dma((count,)), dma((count,)), dma((count,)),
         ],
         compiler_params=pltpu.CompilerParams(
-            collective_id=0, has_side_effects=True, vmem_limit_bytes=48 * 1024 * 1024),
+            collective_id=0, has_side_effects=True, vmem_limit_bytes=63 * 1024 * 1024),
     )(
         state.reshape(nvars, cells, width), axial_speed.reshape(cells, width),
         cross_speed.reshape(2, cells, width), viscosity.reshape(cells, width), coupling,

time: 38.8 us -> 36.5 us (0.941)
  local copies, waits for them, and re-layouts: 5.52 us -> 3.42 us
    unnamed x13 -> x1, local copies, waits for them, and re-layouts: 4.78 us -> 2.1 us
    transpose x1, local copies, waits for them, and re-layouts: 0.75 us -> 1.32 us  [body(): jnp.transpose(targets[0], (2, 0, 1)).reshape(2 * rows, width)]
where the time goes in v2:
time: 36.5 us; the launch traced here: 36.2 us
  Pallas kernels  32.8 us (90%)
  local copies, waits for them, and re-layouts  3.42 us (9%)
    pallas_call x1, Pallas kernels, body(): pl.pallas_call(functools.partial(kernel, count, streams, rads, nvars, pla...  32.8 us
    unnamed x1, local copies, waits for them, and re-layouts  2.1 us
    transpose x1, local copies, waits for them, and re-layouts, body(): jnp.transpose(targets[0], (2, 0, 1)).reshape(2 * rows, width)  1.32 us

profile of v2, /device:TPU:16, one launch (start us, length us, event | category | flops | bytes accessed | tf_op | source)
XLA Modules:
  0.0 36.2 jit_solution(7509273019174100075)
XLA Ops:
  0.0 1.3 %copy.8 = s32[2,16,128]{2,1,0:T(8,128)} copy(s32[2,16,128]{2,0,1:T(2,128)} %bitcast.16) | data formatting | bytes 32768 | tf_op jit(solution)/shard_map/transpose | solution.py:477
  1.3 32.8 %shard_map.73 = f32[6,256,128]{2,1,0:T(8,128)} custom-call(f32[6,256,128]{2,1,0:T(8,128)} %bitcast.11, f32[256,128]{1,0:T(8,128)} %bitcast.13, f32[2,256,128]{2,1,0:T(8,128)} %bitcast.12, f32[256,128]{1,0:T(8,128)} %bitcast.14, f32[6,6]{1,0:T(8,128)} %coupling.1, s32[32,128]{1,0:T(8,128)} %bitcast.15, f32[16,128]{1,0:T(8,128)} %bitcast.17), custom_call_target="tpu_custom_call" | custom-call | tf_op jit(solution)/shard_map/pallas_call | solution.py:449
  34.1 2.1 %copy.10 = f32[1,6,16,16,128]{4,3,2,1,0:T(8,128)} copy(f32[1,6,16,16,128]{4,3,2,1,0:T(8,128)} %bitcast.10) | data formatting | bytes 1572864

commit v3 on v2

--- a/solution.py
+++ b/solution.py
@@ -36,9 +36,9 @@
 def kernel(
     count, streams, rads, nvars, planes, rows, width,
     u, axial, cross_in, viscosity_in, coupling, targets_in, shares_in, out,
-    up, axp, cross, viscosity, targets, shares, wide, xb, cb, f, ur, urs, fr, frs, wv, bs, br, ds, dr,
+    up, axp, cross, viscosity, targets, shares, wide, xb, cb, f, ur, urs, fr, frs, wv, bs, br,
     local_sem, x_send, x_recv, c_send, c_recv, uz_send, uz_recv, fz_send, fz_recv,
-    a_send, a_recv, ur_send, ur_recv, fr_send, fr_recv, b_send, b_recv, d_send, d_recv,
+    a_send, a_recv, ur_send, ur_recv, fr_send, fr_recv, b_send, b_recv,
 ):
     chips = count // 2
     chunks = chunk_list(planes)
@@ -111,10 +111,10 @@
             send_sem=fr_send.at[side, j], recv_sem=fr_recv.at[side, j],
             device_id={"rad": r + 1 if to_high else r - 1}, device_id_type=MESH)
 
-    def face_copy(source, landing, send, recv, m, slot):
-        return pltpu.make_async_remote_copy(
-            src_ref=source.at[m], dst_ref=landing.at[slot],
-            send_sem=send.at[m], recv_sem=recv.at[slot],
+    def face_copy(m, slot):
+        return pltpu.make_async_remote_copy(
+            src_ref=bs.at[m], dst_ref=br.at[slot],
+            send_sem=b_send.at[m], recv_sem=b_recv.at[slot],
             device_id={"inst": m, "stream": z + 1}, device_id_type=MESH)
 
     def local_copies(first=0, last=6):
@@ -213,12 +213,13 @@
     pl.when(has_rhi)(lambda: ur_copy(1).start())
     pl.when(has_rlo)(lambda: ur_copy(0).start())
 
-    def scatter(result):
+    fpad = wv.shape[0] // rows
+
+    def scatter():
         span = min(count, 4) * width
 
-        @pl.loop(0, rows)
-        def _(row):
-            flux = wv[pl.ds(pl.multiple_of(row * vpad, vpad), vpad), :]
+        def one_row(row, _):
+            flux = wv[pl.ds(pl.multiple_of(row * fpad, fpad), fpad), :]
             share = shares[pl.ds(row, 1), :]
             parts = []
             for value in (flux * share, flux * (1.0 - share)):
@@ -227,32 +228,33 @@
                 middle = rest.astype(jnp.bfloat16).astype(jnp.float32)
                 stack = jnp.concatenate([high, middle, rest - middle], axis=0)
                 parts.append(stack.astype(jnp.bfloat16))
+            left = jnp.concatenate(parts, axis=1)
             slots = lax.broadcasted_iota(jnp.int32, (span, width), 0)
             for start in range(0, count * width, span):
-                total = jnp.zeros((3 * vpad, span), jnp.float32)
+                hits = []
                 for k in range(2):
                     target = targets[pl.ds(k * rows + row, 1), :]
-                    hit = (slots + start == target).astype(jnp.float32).astype(jnp.bfloat16)
-                    total = total + lax.dot_general(
-                        parts[k], hit, (((1,), (1,)), ((), ())),
-                        preferred_element_type=jnp.float32)
-                total = total[:vpad] + total[vpad:2 * vpad] + total[2 * vpad:]
+                    hits.append((slots + start == target).astype(jnp.float32).astype(jnp.bfloat16))
+                total = lax.dot_general(
+                    left, jnp.concatenate(hits, axis=1), (((1,), (1,)), ((), ())),
+                    preferred_element_type=jnp.float32)
+                total = total[:fpad] + total[fpad:2 * fpad] + total[2 * fpad:]
                 for i in range(span // width):
-                    wide[start // width + i, pl.ds(pl.multiple_of(row * vpad, vpad), vpad), :] = (
+                    wide[start // width + i, pl.ds(pl.multiple_of(row * fpad, fpad), fpad), :] = (
                         total[:, i * width:(i + 1) * width])
+            return 0
+
+        lax.fori_loop(0, rows, one_row, 0, unroll=2)
 
         for m in range(count):
             for v in range(nvars):
-                result[m, v] = wide[m, pl.ds(v, rows, stride=vpad), :]
-
-    @pl.when(face)
-    def _():
-        speed = axp[rows_of(planes), :]
-        for v in range(nvars):
-            wv[pl.ds(v, rows, stride=vpad), :] = speed * up[v, rows_of(planes), :]
-        scatter(bs)
+                bs[m, v] = wide[m, pl.ds(v, rows, stride=fpad), :]
         for m in range(count):
-            face_copy(bs, br, b_send, b_recv, m, me).start()
+            for v in range(nvars):
+                total = -wide[m, pl.ds(nvars + v, rows, stride=fpad), :]
+                for k in range(1, count):
+                    total = total + (half_step * once[k]) * bs[(m - k) % count, v]
+                bs[m, nvars + v] = total
 
     row_index = lax.broadcasted_iota(jnp.int32, (rows, width), 0)
     first_row, last_row = row_index == 0, row_index == rows - 1
@@ -289,16 +291,17 @@
     pl.when(has_rlo)(lambda: ur_copy(1).wait_recv())
     pl.when(has_rhi)(lambda: ur_copy(0).wait_recv())
 
-    @pl.loop(0, planes)
-    def _(s):
-        here, results = operator(s, up, ur)
-        for v in range(nvars):
-            f[v, row_at(s, 1), :] = here[v] - half_step * results[v]
-
-    def gather(landing, recv):
-        for n in range(count):
-            face_copy(landing, landing, recv, recv, 0, n).wait_recv()
-        return [sum((landing[n, v] for n in range(1, count)), landing[0, v]) for v in range(nvars)]
+    def prepare(start, stop):
+        @pl.loop(start, stop)
+        def _(s):
+            here, results = operator(s, up, ur)
+            for v in range(nvars):
+                f[v, row_at(s, 1), :] = here[v] - half_step * results[v]
+
+    prepare(planes - 1, planes)
+
+    def gather(first):
+        return [sum((br[n, v] for n in range(1, count)), br[0, v]) for v in range(first, first + nvars)]
 
     pairs = [(once[k], once[k] - half_step * twice[k]) for k in range(count)]
     zero_step = lax.convert_element_type(core, jnp.int32) == 0
@@ -316,7 +319,9 @@
         if s0 == 0:
             @pl.when(stator)
             def _():
-                for v, inflow in enumerate(gather(br, b_recv)):
+                for n in range(count):
+                    face_copy(0, n).wait_recv()
+                for v, inflow in enumerate(gather(0)):
                     f[v, rows_of(0, 1, 1), :] += half_step * inflow
 
         for s in range(s0, s0 + n):
@@ -330,11 +335,11 @@
                     combined = combined + g * value
                 new = f[v, rows_of(s, 1, 1), :] - pseudo_step * spectral
                 f[v, rows_of(s, 1, 1), :] = new
-                out[v, rows_of(s), :] = own - pseudo_step * combined
+                out[v, rows_of(s), :] = combined
                 frs[0, s, v:v + 1, :] = new[rows - 1:rows]
                 frs[1, s, v:v + 1, :] = new[0:1]
                 if s == planes - 1:
-                    wv[pl.ds(v, rows, stride=vpad), :] = axp[rows_of(planes), :] * (new + half_step * spectral)
+                    wv[pl.ds(nvars + v, rows, stride=fpad), :] = axp[rows_of(planes), :] * (new + half_step * spectral)
         pl.when(has_rhi)(lambda: fr_copy(1, j).start())
         pl.when(has_rlo)(lambda: fr_copy(0, j).start())
         if s0 == planes - 1:
@@ -342,14 +347,12 @@
 
             @pl.when(face)
             def _():
-                scatter(ds)
+                speed = axp[rows_of(planes), :]
+                for v in range(nvars):
+                    wv[pl.ds(v, rows, stride=fpad), :] = speed * up[v, rows_of(planes), :]
+                scatter()
                 for m in range(count):
-                    total = -ds[m]
-                    for k in range(1, count):
-                        total = total + (half_step * once[k]) * bs[(m - k) % count]
-                    ds[m] = total
-                for m in range(count):
-                    face_copy(ds, dr, d_send, d_recv, m, me).start()
+                    face_copy(m, me).start()
         if s0 == 0:
             pl.when(has_zlo)(lambda: fz_copy(0).start())
 
@@ -358,7 +361,7 @@
         def _(s):
             _, results = operator(s, f, fr)
             for v in range(nvars):
-                out[v, row_at(s), :] -= pseudo_step * results[v]
+                out[v, row_at(s), :] += results[v]
 
     done = {0, planes - 1}
     ready = set()
@@ -382,8 +385,8 @@
 
             @pl.when(stator)
             def _():
-                for v, inflow in enumerate(gather(dr, d_recv)):
-                    out[v, rows_of(0), :] -= pseudo_step * inflow
+                for v, inflow in enumerate(gather(nvars)):
+                    out[v, rows_of(0), :] += inflow
 
     steps = len(chunks)
     for j in range(steps + 2):
@@ -397,6 +400,7 @@
             for later in range(early, steps):
                 for d in range(1, chips):
                     x_copy(d, later).start()
+            prepare(0, planes - 1)
         if 2 <= j:
             finals(j - 2)
 
@@ -432,15 +436,14 @@
     @pl.when(face)
     def _():
         for m in range(count):
-            face_copy(bs, br, b_send, b_recv, m, me).wait_send()
-            face_copy(ds, dr, d_send, d_recv, m, me).wait_send()
+            face_copy(m, me).wait_send()
 
 
 def body(state, axial_speed, cross_speed, viscosity, coupling, targets, shares):
     count, streams, rads = (lax.axis_size(name) for name in ("inst", "stream", "rad"))
     _, nvars, planes, rows, width = state.shape
     chips, chunks = count // 2, len(chunk_list(planes))
-    vpad = -(-nvars // 8) * 8
+    vpad, fpad = -(-nvars // 8) * 8, -(-2 * nvars // 16) * 16
     cells = planes * rows
     vmem = pl.BlockSpec(memory_space=pltpu.VMEM)
     hbm = pl.BlockSpec(memory_space=pltpu.HBM)
@@ -455,19 +458,18 @@
             buf(nvars, cells + 2 * rows, width), buf(cells + rows, width),
             buf(2, cells, width), buf(cells, width),
             pltpu.VMEM((2 * rows, width), jnp.int32), buf(rows, width),
-            buf(count, rows * vpad, width),
+            buf(count, rows * fpad, width),
             buf(chips - 1, nvars, cells, width), buf(chips, nvars, cells, width),
             buf(nvars, cells + 2 * rows, width),
             buf(2, planes, vpad, width), buf(2, planes, vpad, width),
             buf(2, planes, vpad, width), buf(2, planes, vpad, width),
-            buf(rows * vpad, width),
-            buf(count, nvars, rows, width), buf(count, nvars, rows, width),
-            buf(count, nvars, rows, width), buf(count, nvars, rows, width),
+            buf(rows * fpad, width),
+            buf(count, 2 * nvars, rows, width), buf(count, 2 * nvars, rows, width),
             dma((6,)), dma((chips - 1, chunks)), dma((chips - 1, chunks)),
             dma((chips, chunks)), dma((chips, chunks)),
             dma((2,)), dma((2,)), dma((2,)), dma((2,)), dma((1,)), dma((1,)),
             dma((2,)), dma((2,)), dma((2, chunks)), dma((2, chunks)),
-            dma((count,)), dma((count,)), dma((count,)), dma((count,)),
+            dma((count,)), dma((count,)),
         ],
         compiler_params=pltpu.CompilerParams(
             collective_id=0, has_side_effects=True, vmem_limit_bytes=63 * 1024 * 1024),
@@ -476,7 +478,7 @@
         cross_speed.reshape(2, cells, width), viscosity.reshape(cells, width), coupling,
         jnp.transpose(targets[0], (2, 0, 1)).reshape(2 * rows, width), shares[0],
     )
-    return result.reshape(state.shape)
+    return state - pseudo_step * result.reshape(state.shape)
 
 
 def solution(mesh):

time: 36.5 us -> 36.6 us (level)
  other arithmetic: 0 us -> 2.24 us
  local copies, waits for them, and re-layouts: 3.42 us -> 1.43 us
    unnamed x1 -> x2, local copies, waits for them, and re-layouts: 2.1 us -> 0.1 us
    mul x0 -> x1, other arithmetic: none -> 1.26 us  [body(): return state - pseudo_step * result.reshape(state.shape)]
    sub x0 -> x1, other arithmetic: none -> 0.98 us  [body(): return state - pseudo_step * result.reshape(state.shape)]
where the time goes in v3:
time: 36.6 us; the launch traced here: 36.4 us
  Pallas kernels  32.7 us (89%)
  other arithmetic  2.24 us (6%)
  local copies, waits for them, and re-layouts  1.43 us (4%)
    pallas_call x1, Pallas kernels, body(): pl.pallas_call(functools.partial(kernel, count, streams, rads, nvars, pla...  32.7 us
    transpose x1, local copies, waits for them, and re-layouts, body(): jnp.transpose(targets[0], (2, 0, 1)).reshape(2 * rows, width)  1.32 us
    mul x1, other arithmetic, body(): return state - pseudo_step * result.reshape(state.shape)  1.26 us
    sub x1, other arithmetic, body(): return state - pseudo_step * result.reshape(state.shape)  0.98 us

profile of v3, /device:TPU:16, one launch (start us, length us, event | category | flops | bytes accessed | tf_op | source)
XLA Modules:
  0.0 36.4 jit_solution(3556557007406798659)
XLA Ops:
  0.0 1.3 %copy.8 = s32[2,16,128]{2,1,0:T(8,128)} copy(s32[2,16,128]{2,0,1:T(2,128)} %bitcast.16) | data formatting | bytes 32768 | tf_op jit(solution)/shard_map/transpose | solution.py:479
  1.3 32.7 %shard_map.73 = f32[6,256,128]{2,1,0:T(8,128)} custom-call(f32[6,256,128]{2,1,0:T(8,128)} %bitcast.10, f32[256,128]{1,0:T(8,128)} %bitcast.13, f32[2,256,128]{2,1,0:T(8,128)} %bitcast.12, f32[256,128]{1,0:T(8,128)} %bitcast.14, f32[6,6]{1,0:T(8,128)} %coupling.1, s32[32,128]{1,0:T(8,128)} %bitcast.15, f32[16,128]{1,0:T(8,128)} %bitcast.17), custom_call_target="tpu_custom_call" | custom-call | tf_op jit(solution)/shard_map/pallas_call | solution.py:452
  34.0 0.0 copy-start
  34.0 1.3 %broadcast_multiply_fusion = f32[6,256,128]{2,1,0:T(8,128)S(1)} fusion(f32[6,256,128]{2,1,0:T(8,128)} %shard_map.73), kind=kLoop, calls=%fused_computation | loop fusion | flops 196608 | bytes 1572864 | tf_op jit(solution)/shard_map/mul | solution.py:481
  35.3 0.1 copy-done
  35.4 1.0 %sub.3 = f32[1,6,16,16,128]{4,3,2,1,0:T(8,128)} subtract(f32[1,6,16,16,128]{4,3,2,1,0:T(8,128)S(1)} %copy-done, f32[1,6,16,16,128]{4,3,2,1,0:T(8,128)S(1)} %bitcast.11) | non-fusion elementwise | flops 196608 | bytes 2359296 | tf_op jit(solution)/shard_map/sub | solution.py:481
Async XLA Ops:
  34.0 1.4 %copy-start = (f32[1,6,16,16,128]{4,3,2,1,0:T(8,128)S(1)}, f32[1,6,16,16,128]{4,3,2,1,0:T(8,128)}, u32[]{:S(2)}) copy-start(f32[1,6,16,16,128]{4,3,2,1,0:T(8,128)} %param.7) | copy-start | bytes 2359300

commit v4 on v3

--- a/solution.py
+++ b/solution.py
@@ -36,9 +36,9 @@
 def kernel(
     count, streams, rads, nvars, planes, rows, width,
     u, axial, cross_in, viscosity_in, coupling, targets_in, shares_in, out,
-    up, axp, cross, viscosity, targets, shares, wide, xb, cb, f, ur, urs, fr, frs, wv, bs, br,
+    up, axp, cross, viscosity, targets, shares, wide, xb, cb, f, ur, urs, fr, frs, wv, bs, bp, br,
     local_sem, x_send, x_recv, c_send, c_recv, uz_send, uz_recv, fz_send, fz_recv,
-    a_send, a_recv, ur_send, ur_recv, fr_send, fr_recv, b_send, b_recv,
+    a_send, a_recv, ur_send, ur_recv, fr_send, fr_recv, b_send, b_recv, p_send, p_recv,
 ):
     chips = count // 2
     chunks = chunk_list(planes)
@@ -111,11 +111,17 @@
             send_sem=fr_send.at[side, j], recv_sem=fr_recv.at[side, j],
             device_id={"rad": r + 1 if to_high else r - 1}, device_id_type=MESH)
 
-    def face_copy(m, slot):
-        return pltpu.make_async_remote_copy(
-            src_ref=bs.at[m], dst_ref=br.at[slot],
-            send_sem=b_send.at[m], recv_sem=b_recv.at[slot],
-            device_id={"inst": m, "stream": z + 1}, device_id_type=MESH)
+    def pair_copy(q):
+        return pltpu.make_async_remote_copy(
+            src_ref=bs.at[2 * q + 1 - core], dst_ref=bp.at[q],
+            send_sem=p_send.at[q], recv_sem=p_recv.at[q],
+            device_id={"inst": peer}, device_id_type=MESH)
+
+    def face_copy(q, slot):
+        return pltpu.make_async_remote_copy(
+            src_ref=bs.at[2 * q + core], dst_ref=br.at[slot],
+            send_sem=b_send.at[q], recv_sem=b_recv.at[slot],
+            device_id={"inst": 2 * q + core, "stream": z + 1}, device_id_type=MESH)
 
     def local_copies(first=0, last=6):
         pairs = [
@@ -301,7 +307,7 @@
     prepare(planes - 1, planes)
 
     def gather(first):
-        return [sum((br[n, v] for n in range(1, count)), br[0, v]) for v in range(first, first + nvars)]
+        return [sum((br[n, v] for n in range(1, chips)), br[0, v]) for v in range(first, first + nvars)]
 
     pairs = [(once[k], once[k] - half_step * twice[k]) for k in range(count)]
     zero_step = lax.convert_element_type(core, jnp.int32) == 0
@@ -319,7 +325,7 @@
         if s0 == 0:
             @pl.when(stator)
             def _():
-                for n in range(count):
+                for n in range(chips):
                     face_copy(0, n).wait_recv()
                 for v, inflow in enumerate(gather(0)):
                     f[v, rows_of(0, 1, 1), :] += half_step * inflow
@@ -335,7 +341,7 @@
                     combined = combined + g * value
                 new = f[v, rows_of(s, 1, 1), :] - pseudo_step * spectral
                 f[v, rows_of(s, 1, 1), :] = new
-                out[v, rows_of(s), :] = combined
+                out[v, rows_of(s), :] = pseudo_step * combined
                 frs[0, s, v:v + 1, :] = new[rows - 1:rows]
                 frs[1, s, v:v + 1, :] = new[0:1]
                 if s == planes - 1:
@@ -351,8 +357,14 @@
                 for v in range(nvars):
                     wv[pl.ds(v, rows, stride=fpad), :] = speed * up[v, rows_of(planes), :]
                 scatter()
-                for m in range(count):
-                    face_copy(m, me).start()
+                for q in range(chips):
+                    pair_copy(q).start()
+                for q in range(chips):
+                    pair_copy(q).wait_recv()
+                    slot = 2 * q + core
+                    for v in range(2 * nvars):
+                        bs[slot, v] = bs[slot, v] + bp[q, v]
+                    face_copy(q, chip).start()
         if s0 == 0:
             pl.when(has_zlo)(lambda: fz_copy(0).start())
 
@@ -361,7 +373,7 @@
         def _(s):
             _, results = operator(s, f, fr)
             for v in range(nvars):
-                out[v, row_at(s), :] += results[v]
+                out[v, row_at(s), :] += pseudo_step * results[v]
 
     done = {0, planes - 1}
     ready = set()
@@ -386,7 +398,7 @@
             @pl.when(stator)
             def _():
                 for v, inflow in enumerate(gather(nvars)):
-                    out[v, rows_of(0), :] += inflow
+                    out[v, rows_of(0), :] += pseudo_step * inflow
 
     steps = len(chunks)
     for j in range(steps + 2):
@@ -435,8 +447,9 @@
 
     @pl.when(face)
     def _():
-        for m in range(count):
-            face_copy(m, me).wait_send()
+        for q in range(chips):
+            pair_copy(q).wait_send()
+            face_copy(q, chip).wait_send()
 
 
 def body(state, axial_speed, cross_speed, viscosity, coupling, targets, shares):
@@ -464,12 +477,12 @@
             buf(2, planes, vpad, width), buf(2, planes, vpad, width),
             buf(2, planes, vpad, width), buf(2, planes, vpad, width),
             buf(rows * fpad, width),
-            buf(count, 2 * nvars, rows, width), buf(count, 2 * nvars, rows, width),
+            buf(count, 2 * nvars, rows, width), buf(chips, 2 * nvars, rows, width), buf(chips, 2 * nvars, rows, width),
             dma((6,)), dma((chips - 1, chunks)), dma((chips - 1, chunks)),
             dma((chips, chunks)), dma((chips, chunks)),
             dma((2,)), dma((2,)), dma((2,)), dma((2,)), dma((1,)), dma((1,)),
             dma((2,)), dma((2,)), dma((2, chunks)), dma((2, chunks)),
-            dma((count,)), dma((count,)),
+            dma((chips,)), dma((chips,)), dma((chips,)), dma((chips,)),
         ],
         compiler_params=pltpu.CompilerParams(
             collective_id=0, has_side_effects=True, vmem_limit_bytes=63 * 1024 * 1024),
@@ -478,7 +491,7 @@
         cross_speed.reshape(2, cells, width), viscosity.reshape(cells, width), coupling,
         jnp.transpose(targets[0], (2, 0, 1)).reshape(2 * rows, width), shares[0],
     )
-    return state - pseudo_step * result.reshape(state.shape)
+    return state - result.reshape(state.shape)
 
 
 def solution(mesh):

time: 36.6 us -> 34.4 us (0.940)
  Pallas kernels: 32.7 us -> 30.7 us
    pallas_call x1, Pallas kernels: 32.7 us -> 30.7 us  [body(): pl.pallas_call(functools.partial(kernel, count, streams, rads, nvars, pla...]
    mul x1 -> x0, other arithmetic: 1.26 us -> none  [body(): return state - pseudo_step * result.reshape(state.shape)]
    sub x1, other arithmetic: 0.98 us -> 2.12 us  [body(): return state - result.reshape(state.shape)]
where the time goes in v4:
time: 34.4 us; the launch traced here: 34.2 us
  Pallas kernels  30.7 us (89%)
  other arithmetic  2.12 us (6%)
  local copies, waits for them, and re-layouts  1.33 us (4%)
    pallas_call x1, Pallas kernels, body(): pl.pallas_call(functools.partial(kernel, count, streams, rads, nvars, pla...  30.7 us
    sub x1, other arithmetic, body(): return state - result.reshape(state.shape)  2.12 us
    transpose x1, local copies, waits for them, and re-layouts, body(): jnp.transpose(targets[0], (2, 0, 1)).reshape(2 * rows, width)  1.32 us

profile of v4, /device:TPU:16, one launch (start us, length us, event | category | flops | bytes accessed | tf_op | source)
XLA Modules:
  0.0 34.2 jit_solution(15425116266793814117)
XLA Ops:
  0.0 1.3 %copy.8 = s32[2,16,128]{2,1,0:T(8,128)} copy(s32[2,16,128]{2,0,1:T(2,128)} %bitcast.16) | data formatting | bytes 32768 | tf_op jit(solution)/shard_map/transpose | solution.py:492
  1.3 0.0 copy-start
  1.3 30.7 %shard_map.73 = f32[6,256,128]{2,1,0:T(8,128)} custom-call(f32[6,256,128]{2,1,0:T(8,128)} %bitcast.10, f32[256,128]{1,0:T(8,128)} %bitcast.13, f32[2,256,128]{2,1,0:T(8,128)} %bitcast.12, f32[256,128]{1,0:T(8,128)} %bitcast.14, f32[6,6]{1,0:T(8,128)} %coupling.1, s32[32,128]{1,0:T(8,128)} %bitcast.15, f32[16,128]{1,0:T(8,128)} %bitcast.17), custom_call_target="tpu_custom_call" | custom-call | tf_op jit(solution)/shard_map/pallas_call | solution.py:465
  32.0 0.0 copy-done
  32.1 2.1 %sub.3 = f32[1,6,16,16,128]{4,3,2,1,0:T(8,128)} subtract(f32[1,6,16,16,128]{4,3,2,1,0:T(8,128)S(1)} %copy-done, f32[1,6,16,16,128]{4,3,2,1,0:T(8,128)} %bitcast.11) | non-fusion elementwise | flops 196608 | bytes 2359296 | tf_op jit(solution)/shard_map/sub | solution.py:494
Async XLA Ops:
  1.3 30.7 %copy-start = (f32[1,6,16,16,128]{4,3,2,1,0:T(8,128)S(1)}, f32[1,6,16,16,128]{4,3,2,1,0:T(8,128)}, u32[]{:S(2)}) copy-start(f32[1,6,16,16,128]{4,3,2,1,0:T(8,128)} %param.7) | copy-start | bytes 2359300
